TPU v7x, 32 devices: a whole 2x2x4 slice. The times are simulated.
32 devices in a mesh: rows: 16 (over z, y, core), chan: 2 (over x).
Axes of the slice: x: 2, y: 2, z: 4, core: 2. Of those that a mesh axis runs over, the one named last changes fastest.
Arguments:
- pair: bfloat16 [128, 128, 128], P('rows', 'chan'), may hold values from -6 to 6
- block_mask: int32 [1, 1], replicated, may hold values from 0 to 1, as said below
- w_in: bfloat16 [128, 640], replicated, may hold values from -0.5 to 0.5
- w_out: bfloat16 [128, 128], replicated, may hold values from -0.5 to 0.5
Outputs:
- update: bfloat16 [128, 128, 128], P('rows', 'chan')
Inputs may be any that keep to these rules, and one draw needn't show every extreme that they name: Every diagonal entry of block_mask is 1; other entries are 0 or 1.
All inputs are finite; a program needn't handle non-finite values.
Results may differ from a plain program's by a relative error of at most 0.0078.
Values may be sent and summed in bfloat16 or wider, within the bound.
No kernel may reach another device: no remote copies, remote signals or barrier semaphores. Data moves between devices by JAX's collectives and lax.ppermute only.
A program may use at most 64 MiB of HBM per device.

v0:
```python
import jax
import jax.numpy as jnp
from jax import lax
from jax.sharding import PartitionSpec as P

BLOCK = 128


def layer_norm(values):
    mean = jnp.mean(values, axis=-1, keepdims=True)
    centered = values - mean
    var = jnp.mean(centered * centered, axis=-1, keepdims=True)
    return centered / jnp.sqrt(var + 1e-05)


def channel_product(left, piece):
    return jnp.einsum("cik,cjk->cij", left, piece, preferred_element_type=jnp.float32)


def on_device(pair, block_mask, w_in, w_out):
    rows_dev, cols_dev, width = pair.shape
    n_blocks = block_mask.shape[0]
    row_start = lax.axis_index("rows") * rows_dev
    col_start = lax.axis_index("chan") * cols_dev
    row_ids = row_start + lax.broadcasted_iota(jnp.int32, (rows_dev, n_blocks), 0)
    col_ids = col_start + lax.broadcasted_iota(jnp.int32, (cols_dev, n_blocks), 0)
    rows_hot = (
        row_ids // BLOCK == lax.broadcasted_iota(jnp.int32, (rows_dev, n_blocks), 1)
    ).astype(jnp.float32)
    cols_hot = (
        col_ids // BLOCK == lax.broadcasted_iota(jnp.int32, (cols_dev, n_blocks), 1)
    ).astype(jnp.float32)
    mask_float = block_mask.astype(jnp.float32)
    local_mask = jnp.dot(jnp.dot(rows_hot, mask_float), cols_hot.T)[:, :, None]
    normed = layer_norm(pair.astype(jnp.float32)).astype(jnp.bfloat16)
    proj = jnp.dot(normed.reshape(-1, width), w_in, preferred_element_type=jnp.float32).reshape(
        rows_dev, cols_dev, 5 * width
    )
    left = (jax.nn.sigmoid(proj[..., :width]) * proj[..., width : 2 * width] * local_mask).astype(
        jnp.bfloat16
    )
    right = (
        jax.nn.sigmoid(proj[..., 2 * width : 3 * width])
        * proj[..., 3 * width : 4 * width]
        * local_mask
    ).astype(jnp.bfloat16)
    gate = jax.nn.sigmoid(proj[..., 4 * width :])
    left_t = jnp.transpose(left, (2, 0, 1))
    right_t = jnp.transpose(right, (2, 0, 1))
    left_ch, right_ch = (
        lax.all_to_all(left_t, "chan", split_axis=0, concat_axis=2, tiled=True),
        lax.all_to_all(right_t, "chan", split_axis=0, concat_axis=2, tiled=True),
    )
    prod_ch = channel_product(left_ch, lax.all_gather(right_ch, "rows", axis=1, tiled=True))
    prod_back = lax.all_to_all(prod_ch, "chan", split_axis=2, concat_axis=0, tiled=True)
    prod = jnp.transpose(prod_back, (1, 2, 0))
    normed_prod = layer_norm(prod).astype(jnp.bfloat16)
    mixed = jnp.dot(
        normed_prod.reshape(-1, width), w_out, preferred_element_type=jnp.float32
    ).reshape(rows_dev, cols_dev, width)
    return (gate * mixed).astype(jnp.bfloat16)


def solution(mesh):
    placed = (P("rows", "chan", None), P(), P(), P())
    return jax.shard_map(
        on_device, mesh=mesh, in_specs=placed, out_specs=P("rows", "chan", None), check_vma=False
    )
```

profile of v0, /device:TPU:0, one launch (start us, length us, event | category | flops | bytes accessed | tf_op | source)
XLA Modules:
  0.0 85.9 jit_solution(8885466216950798862)
XLA Ops:
  6.5 0.0 copy-start
  6.5 0.0 all-gather.2.cloned.1.call-start
  6.5 1.1 %convert_reduce_fusion = f32[8,64]{1,0:T(8,128)S(1)} fusion(bf16[8,64,128]{2,1,0:T(8,128)(2,1)} %param.4), kind=kLoop, calls=%fused_computation.3 | loop fusion | flops 130560 | bytes 133120 | tf_op jit(solution)/shard_map/reduce_sum | solution.py:10
  7.6 1.2 %fusion.3 = f32[8,64]{1,0:T(8,128)S(1)} fusion(bf16[8,64,128]{2,1,0:T(8,128)(2,1)} %param.4, f32[8,64]{1,0:T(8,128)S(1)} %broadcast_multiply_fusion.2), kind=kLoop, calls=%fused_computation.6 | loop fusion | flops 261632 | bytes 135168 | tf_op jit(solution)/shard_map/reduce_sum | solution.py:12
  9.5 0.0 copy-done
  9.5 1.3 %fusion.18 = f32[8,64,640]{2,1,0:T(8,128)S(1)} fusion(bf16[128,640]{1,0:T(8,128)(2,1)S(1)} %copy-done, bf16[8,64,128]{2,1,0:T(8,128)(2,1)} %param.4, f32[8,64]{1,0:T(8,128)S(1)} %add_sqrt_fusion.1, f32[8,64]{1,0:T(8,128)S(1)} %broadcast_multiply_fusion.2), kind=kOutput, calls=%fused_computation.32 | convolution fusion | flops 84148224 | bytes 1609728 | tf_op jit(solution)/shard_map/dot_general | solution.py:36
  10.8 0.1 broadcast_multiply_fusion
  10.9 0.2 fusion.26
  11.1 0.2 copy.16
  11.3 0.2 reshape.175
  11.5 8.5 %all_to_all.54 = bf16[2,2,16384]{2,1,0:T(2,128)(2,1)S(1)} all-to-all(bf16[2,2,16384]{2,1,0:T(2,128)(2,1)S(1)} %reshape.175), channel_id=1, replica_groups=mesh['rows'=16,'chan'=2] {'chan'}, dimensions={0} | all-to-all | bytes 262144 | tf_op jit(solution)/shard_map/all_to_all | solution.py:52
  20.0 0.2 reshape.176
  20.2 0.3 copy.22
  20.5 0.8 all_to_all.46
  21.3 0.0 all-gather.2.cloned.1.call-update
  21.3 0.2 copy.14
  21.5 0.2 reshape.173
  21.8 6.8 %all_to_all.55 = bf16[2,2,16384]{2,1,0:T(2,128)(2,1)S(1)} all-to-all(bf16[2,2,16384]{2,1,0:T(2,128)(2,1)S(1)} %reshape.173), channel_id=1, replica_groups=mesh['rows'=16,'chan'=2] {'chan'}, dimensions={0} | all-to-all | bytes 262144 | tf_op jit(solution)/shard_map/all_to_all | solution.py:51
  28.6 0.2 reshape.174
  28.9 0.3 copy.23
  29.1 0.1 all_to_all.42
  29.3 33.7 %all-gather.2.cloned.1.call-done = bf16[64,128,128]{2,1,0:T(8,128)(2,1)} async-done(((bf16[64,8,128]{2,1,0:T(8,128)(2,1)}), bf16[64,128,128]{2,1,0:T(8,128)(2,1)}) %all-gather.2.cloned.1.call-update) | async-done | bytes 2097168 | tf_op jit(solution)/shard_map/all_gather | solution.py:54
  63.0 2.8 %fusion.29 = f32[64,8,128]{2,1,0:T(8,128)S(1)} fusion(bf16[64,8,128]{2,1,0:T(8,128)(2,1)S(1)} %all_to_all.42, bf16[64,128,128]{2,1,0:T(8,128)(2,1)} %all-gather.2.cloned.1.call-done), kind=kOutput, calls=%fused_computation.57 | convolution fusion | flops 16777216 | bytes 2490368 | tf_op jit(solution)/shard_map/cik,cjk->cij/dot_general | solution.py:17
  65.8 0.3 copy.18
  66.1 0.3 reshape.177
  66.4 0.0 copy-start.1
  66.4 8.3 %all_to_all.56 = f32[2,1,32768]{2,1,0:T(1,128)S(1)} all-to-all(f32[2,1,32768]{2,1,0:T(1,128)S(1)} %reshape.177), channel_id=1, replica_groups=mesh['rows'=16,'chan'=2] {'chan'}, dimensions={0} | all-to-all | bytes 524288 | tf_op jit(solution)/shard_map/all_to_all | solution.py:55
  74.7 0.5 broadcast.296
  75.2 1.4 %reduce = f32[2,32768]{1,0:T(2,128)S(1)} reduce(f32[2,1,32768]{2,1,0:T(1,128)S(1)} %all_to_all.56, f32[]{:T(128)} %broadcast.296), dimensions={1}, to_apply=%all_to_all.47.reduce_sub_computation | reduce | bytes 524292 | tf_op jit(solution)/shard_map/all_to_all | solution.py:55
  76.6 0.3 reshape.178
  77.0 0.4 copy.19
  77.4 0.3 all_to_all.50
  77.7 0.1 bitcast_reduce_fusion
  77.8 0.3 multiply_reduce_fusion
  78.1 0.0 copy-done.1
  78.1 1.0 %fusion = bf16[8,64,128]{2,1,0:T(8,128)(2,1)} fusion(f32[8,64,640]{2,1,0:T(8,128)S(1)} %fusion.18, f32[128,8,64]{0,2,1:T(8,128)S(1)} %all_to_all.50, f32[8,64]{1,0:T(8,128)S(1)} %add_sqrt_fusion, f32[8,64]{1,0:T(8,128)S(1)} %broadcast_multiply_fusion.1, bf16[128,128]{1,0:T(8,128)(2,1)S(1)} %copy-done.1), kind=kOutput, calls=%fused_computation.1 | convolution fusion | flops 17301504 | bytes 692224 | tf_op jit(solution)/shard_map/dot_general | solution.py:58
  (6 shorter events, 0.1 us)
Async XLA Ops:
  6.5 3.0 %copy-start = (bf16[128,640]{1,0:T(8,128)(2,1)S(1)}, bf16[128,640]{1,0:T(8,128)(2,1)}, u32[]{:S(2)}) copy-start(bf16[128,640]{1,0:T(8,128)(2,1)} %param.6) | copy-start | bytes 491524
  6.5 56.5 %all-gather.2.cloned.1.call-start = ((), (), s32[]{:S(2)}) async-start(), calls=%async_computation.3 | async-start | bytes 2228224 | tf_op jit(solution)/shard_map/all_gather | solution.py:54
  66.4 11.7 %copy-start.1 = (bf16[128,128]{1,0:T(8,128)(2,1)S(1)}, bf16[128,128]{1,0:T(8,128)(2,1)}, u32[]{:S(2)}) copy-start(bf16[128,128]{1,0:T(8,128)(2,1)} %param.7) | copy-start | bytes 98308
Sparse Core Ops, SparseCore 0:
  21.5 41.5 all-gather.1
where the time goes:
time: 86.3 us; the launch traced here: 85.9 us
  waiting for transfers between devices  33.7 us (39%)
  blocking collectives  23.6 us (27%)
  between operations  14.2 us (16%)
  matrix products  5.03 us (6%)
  local copies, waits for them, and re-layouts  4.97 us (6%)
  other arithmetic  4.38 us (5%)
    all_gather x1, waiting for transfers between devices, on_device(): lax.all_gather(right_ch, 'rows', axis=1, tiled=True)  33.7 us
    all_to_all x1, blocking collectives, on_device(): lax.all_to_all(right_t, 'chan', split_axis=0, concat_axis=2, tiled=True)  8.48 us
    all_to_all x1, blocking collectives, on_device(): lax.all_to_all(prod_ch, 'chan', split_axis=2, concat_axis=0, tiled=True)  8.26 us
    all_to_all x1, blocking collectives, on_device(): lax.all_to_all(left_t, 'chan', split_axis=0, concat_axis=2, tiled=True)  6.85 us
    dot_general x1, matrix products, channel_product(): jnp.einsum('cik,cjk->cij', left, piece, preferred_element_type=jnp.float32)  2.75 us
  transfers between devices with their start and end apart: 1, of which 1 were waited for; matrix products, arithmetic and copies ran while one was open for 1% of the time, Pallas kernels for 0%

commit v1 on v0

--- a/solution.py
+++ b/solution.py
@@ -1,23 +1,29 @@
 import jax
 import jax.numpy as jnp
 from jax import lax
+from jax.experimental import pallas as pl
+from jax.experimental.pallas import tpu as pltpu
 from jax.sharding import PartitionSpec as P
 
 BLOCK = 128
+LANES = 128
+SUBLANES = 8
+EPS = 1e-05
+AXES = ("rows", "chan")
 
 
 def layer_norm(values):
     mean = jnp.mean(values, axis=-1, keepdims=True)
     centered = values - mean
     var = jnp.mean(centered * centered, axis=-1, keepdims=True)
-    return centered / jnp.sqrt(var + 1e-05)
+    return centered / jnp.sqrt(var + EPS)
 
 
 def channel_product(left, piece):
     return jnp.einsum("cik,cjk->cij", left, piece, preferred_element_type=jnp.float32)
 
 
-def on_device(pair, block_mask, w_in, w_out):
+def gathered(pair, block_mask, w_in, w_out):
     rows_dev, cols_dev, width = pair.shape
     n_blocks = block_mask.shape[0]
     row_start = lax.axis_index("rows") * rows_dev
@@ -61,7 +67,169 @@
     return (gate * mixed).astype(jnp.bfloat16)
 
 
+def dot_t(a, b, contract):
+    return lax.dot_general(a, b, ((contract[:1], contract[1:]), ((), ())), preferred_element_type=jnp.float32)
+
+
+def first_half(shape):
+    return lax.broadcasted_iota(jnp.int32, shape, len(shape) - 1) < LANES // 2
+
+
+def swap(values):
+    return pltpu.roll(values, LANES // 2, values.ndim - 1)
+
+
+def project_kernel(mask_ref, pair_ref, w_ref, out_ref, gate_ref, parts):
+    rows_dev, cols_dev, width = pair_ref.shape
+    tokens, half = rows_dev * cols_dev, width // 2
+    row_block = lax.axis_index("rows") * rows_dev // BLOCK
+    col_block = lax.axis_index("chan") * cols_dev // BLOCK
+    half_mask = 0.5 * mask_ref[row_block, col_block].astype(jnp.float32)
+
+    pair = pair_ref[...].reshape(tokens, width)
+    ones = jnp.ones((width, width), jnp.bfloat16)
+    mean = jnp.dot(pair, ones, preferred_element_type=jnp.float32) * (1.0 / width)
+    centered = pair.astype(jnp.float32) - mean
+    square = centered * centered
+    high = square.astype(jnp.bfloat16)
+    low = (square - high.astype(jnp.float32)).astype(jnp.bfloat16)
+    total = jnp.dot(high, ones, preferred_element_type=jnp.float32) + jnp.dot(
+        low, ones, preferred_element_type=jnp.float32
+    )
+    normed = (centered * lax.rsqrt(total * (1.0 / width) + EPS)).astype(jnp.bfloat16)
+
+    pick = first_half((half, LANES))
+    for side in range(2):
+        begin = 2 * side * width
+        gates = dot_t(w_ref[:, begin : begin + width], normed, (0, 1))
+        values = dot_t(w_ref[:, begin + width : begin + 2 * width], normed, (0, 1))
+        held = (jnp.tanh(0.5 * gates) * half_mask + half_mask) * values
+        for at in range(tokens // LANES):
+            low_c = held[:half, at * LANES : (at + 1) * LANES]
+            high_c = held[half:, at * LANES : (at + 1) * LANES]
+            parts[side, :, 2 * at, :] = jnp.where(pick, low_c, swap(high_c))
+            parts[side, :, 2 * at + 1, :] = jnp.where(pick, swap(low_c), high_c)
+    n_dev, slab = out_ref.shape[0], out_ref.shape[1] // 2
+    for side in range(2):
+        out_ref[:, side * slab : (side + 1) * slab, :] = (
+            parts[side].reshape(n_dev, slab, LANES).astype(jnp.bfloat16)
+        )
+    gate = jnp.dot(normed, w_ref[:, 4 * width :], preferred_element_type=jnp.float32)
+    gate_ref[...] = 0.5 * jnp.tanh(0.5 * gate) + 0.5
+
+
+def product_kernel(in_ref, out_ref):
+    n_rows, n_chan, slabs, _ = in_ref.shape
+    slab = slabs // 2
+    groups = slab // SUBLANES
+    tokens = n_rows * SUBLANES
+
+    def side(at):
+        values = in_ref[:, :, at * slab : (at + 1) * slab, :].astype(jnp.float32)
+        return values.reshape(n_rows, n_chan, groups, SUBLANES, LANES)
+
+    left, right = side(0), side(1)
+    pick = first_half((tokens, LANES))
+    made = []
+    for g in range(groups):
+        a = [left[:, x, g].reshape(tokens, LANES) for x in range(n_chan)]
+        b = [right[:, x, g].reshape(tokens, LANES) for x in range(n_chan)]
+        rows = [
+            jnp.concatenate([jnp.where(pick, v, 0.0) for v in a], axis=1),
+            jnp.concatenate([jnp.where(pick, 0.0, v) for v in a], axis=1),
+        ]
+        a = jnp.concatenate(rows, axis=0).astype(jnp.bfloat16)
+        b = jnp.concatenate(b, axis=1).astype(jnp.bfloat16)
+        prod = dot_t(a, b, (1, 1))
+        made.append((prod[:tokens], prod[tokens:]))
+    blocks = [
+        [jnp.where(pick, low, swap(high)) for low, high in made],
+        [jnp.where(pick, swap(low), high) for low, high in made],
+    ]
+    for x in range(n_chan):
+        block = jnp.concatenate([v.reshape(n_rows, SUBLANES, LANES) for v in blocks[x]], axis=1)
+        out_ref[:, x] = block.astype(jnp.bfloat16)
+
+
+def finish_kernel(prod_ref, gate_ref, w_ref, out_ref, parts):
+    n_dev, slab, _ = prod_ref.shape
+    rows_dev, cols_dev, width = out_ref.shape
+    prod = prod_ref[...].astype(jnp.float32).reshape(n_dev * slab // SUBLANES, SUBLANES, LANES)
+    total = jnp.sum(prod, axis=0)
+    mean = (total + swap(total)) * (1.0 / width)
+    centered = prod - mean
+    total = jnp.sum(centered * centered, axis=0)
+    var = (total + swap(total)) * (1.0 / width)
+    parts[...] = centered * lax.rsqrt(var + EPS)
+    pick = first_half((width // 2, LANES))
+    w = w_ref[...]
+    for at in range(rows_dev // 2):
+        even, odd = parts[:, 2 * at, :], parts[:, 2 * at + 1, :]
+        normed = jnp.concatenate(
+            [jnp.where(pick, even, swap(odd)), jnp.where(pick, swap(even), odd)], axis=0
+        ).astype(jnp.bfloat16)
+        mixed = dot_t(normed, w, (0, 0))
+        update = gate_ref[at * LANES : (at + 1) * LANES, :] * mixed
+        out_ref[2 * at : 2 * at + 2] = update.astype(jnp.bfloat16).reshape(2, cols_dev, width)
+
+
+def vmem():
+    return pl.BlockSpec(memory_space=pltpu.VMEM)
+
+
+def tiled(n_rows, n_chan, pair, block_mask, w_in, w_out):
+    rows_dev, cols_dev, width = pair.shape
+    n_dev = n_rows * n_chan
+    groups = width // (2 * n_dev)
+    slab = groups * SUBLANES
+    sent, gate = pl.pallas_call(
+        project_kernel,
+        out_shape=(
+            jax.ShapeDtypeStruct((n_dev, 2 * slab, LANES), jnp.bfloat16),
+            jax.ShapeDtypeStruct((rows_dev * cols_dev, width), jnp.float32),
+        ),
+        in_specs=[pl.BlockSpec(memory_space=pltpu.SMEM), vmem(), vmem()],
+        out_specs=(vmem(), vmem()),
+        scratch_shapes=[pltpu.VMEM((2, width // 2, SUBLANES, LANES), jnp.float32)],
+        name="project",
+    )(block_mask, pair, w_in)
+    got = lax.all_to_all(sent, AXES, split_axis=0, concat_axis=0, tiled=True)
+    prod = pl.pallas_call(
+        product_kernel,
+        out_shape=jax.ShapeDtypeStruct((n_rows, n_chan, slab, LANES), jnp.bfloat16),
+        in_specs=[vmem()],
+        out_specs=vmem(),
+        name="product",
+    )(got.reshape(n_rows, n_chan, 2 * slab, LANES))
+    back = lax.all_to_all(
+        prod.reshape(n_dev, slab, LANES), AXES, split_axis=0, concat_axis=0, tiled=True
+    )
+    return pl.pallas_call(
+        finish_kernel,
+        out_shape=jax.ShapeDtypeStruct(pair.shape, jnp.bfloat16),
+        in_specs=[vmem()] * 3,
+        out_specs=vmem(),
+        scratch_shapes=[pltpu.VMEM((width // 2, SUBLANES, LANES), jnp.float32)],
+        name="finish",
+    )(back, gate, w_out)
+
+
 def solution(mesh):
+    n_rows, n_chan = mesh.shape["rows"], mesh.shape["chan"]
+
+    def on_device(pair, block_mask, w_in, w_out):
+        rows_dev, cols_dev, width = pair.shape
+        fits = (
+            n_chan == 2
+            and rows_dev == SUBLANES
+            and 2 * cols_dev == LANES
+            and width == LANES
+            and width % (4 * n_rows * n_chan) == 0
+        )
+        if fits:
+            return tiled(n_rows, n_chan, pair, block_mask, w_in, w_out)
+        return gathered(pair, block_mask, w_in, w_out)
+
     placed = (P("rows", "chan", None), P(), P(), P())
     return jax.shard_map(
         on_device, mesh=mesh, in_specs=placed, out_specs=P("rows", "chan", None), check_vma=False

time: 86.3 us -> 37.9 us (0.44)
  waiting for transfers between devices: 33.7 us -> 0 us
  between operations: 14.2 us -> 0.65 us
  Pallas kernels: 0 us -> 6.99 us
  blocking collectives: 23.6 us -> 30 us
  matrix products: 5.03 us -> 0 us
  local copies, waits for them, and re-layouts: 4.97 us -> 0 us
  other arithmetic: 4.38 us -> 0 us
    all_gather x1 -> x0, waiting for transfers between devices: 33.7 us -> none  [on_device(): lax.all_gather(right_ch, 'rows', axis=1, tiled=True)]
    pallas_call x0 -> x3, Pallas kernels: none -> 6.99 us  [the longest x1 2.76 us: tiled(): pl.pallas_call(project_kernel, out_shape=(jax.ShapeDtypeStruct((n_dev, 2...]
    all_to_all x3 -> x2, blocking collectives: 23.6 us -> 30 us  [the longest x1 18.1 us: tiled(): got = lax.all_to_all(sent, AXES, split_axis=0, concat_axis=0, tiled=True)]
    dot_general x3 -> x0, matrix products: 5.03 us -> none  [the longest x1 2.75 us: channel_product(): jnp.einsum('cik,cjk->cij', left, piece, preferred_element_type=jnp.float32)]
    all_to_all x7 -> x0, local copies, waits for them, and re-layouts: 2.71 us -> none  [the longest x3 1.21 us: on_device(): lax.all_to_all(prod_ch, 'chan', split_axis=2, concat_axis=0, tiled=True)]
    reduce_sum x4 -> x0, other arithmetic: 2.65 us -> none  [the longest x2 1.43 us: layer_norm(): var = jnp.mean(centered * centered, axis=-1, keepdims=True)]
    unnamed x10 -> x0, local copies, waits for them, and re-layouts: 1.59 us -> none
    all_to_all x1 -> x0, other arithmetic: 1.44 us -> none  [on_device(): lax.all_to_all(prod_ch, 'chan', split_axis=2, concat_axis=0, tiled=True)]
  transfers between devices with their start and end apart: 1 -> 0, of which waited for: 1 -> 0; matrix products, arithmetic and copies ran while one was open for 1% -> 0% of each run, Pallas kernels for 0% -> 0%
where the time goes in v1:
time: 37.9 us; the launch traced here: 37.6 us
  blocking collectives  30 us (79%)
  Pallas kernels  6.99 us (18%)
  between operations  0.65 us (2%)
    all_to_all x1, blocking collectives, tiled(): got = lax.all_to_all(sent, AXES, split_axis=0, concat_axis=0, tiled=True)  18.1 us
    all_to_all x1, blocking collectives, tiled(): lax.all_to_all(prod.reshape(n_dev, slab, LANES), AXES, split_axis=0, conc...  11.9 us
    pallas_call x1, Pallas kernels, tiled(): pl.pallas_call(project_kernel, out_shape=(jax.ShapeDtypeStruct((n_dev, 2...  2.76 us
    pallas_call x1, Pallas kernels, tiled(): pl.pallas_call(finish_kernel, out_shape=jax.ShapeDtypeStruct(pair.shape,...  2.32 us
    pallas_call x1, Pallas kernels, tiled(): pl.pallas_call(product_kernel, out_shape=jax.ShapeDtypeStruct((n_rows, n_...  1.91 us

profile of v1, /device:TPU:0, one launch (start us, length us, event | category | flops | bytes accessed | tf_op | source)
XLA Modules:
  0.0 37.6 jit_solution(3631826662238481886)
XLA Ops:
  0.7 2.8 %project.1 = (bf16[32,32,128]{2,1,0:T(8,128)(2,1)}, f32[512,128]{1,0:T(8,128)}) custom-call(s32[1,1]{1,0:T(1,128)S(6)} %copy.5.mask_ref, bf16[8,64,128]{2,1,0:T(8,128)(2,1)} %pair_ref.1, bf16[128,640]{1,0:T(8,128)(2,1)} %w_ref.2), custom_call_target="tpu_custom_call" | custom-call | tf_op jit(solution)/shard_map/project/pallas_call | solution.py:185
  3.4 18.1 %all_to_all.10 = bf16[32,32,128]{2,1,0:T(8,128)(2,1)} all-to-all(bf16[32,32,128]{2,1,0:T(8,128)(2,1)} %get-tuple-element.7), channel_id=1, replica_groups=mesh['rows'=16,'chan'=2] {'rows','chan'}, dimensions={0} | all-to-all | bytes 524288 | tf_op jit(solution)/shard_map/all_to_all | solution.py:196
  21.5 1.9 %product.1 = bf16[16,2,16,128]{3,2,1,0:T(8,128)(2,1)} custom-call(bf16[16,2,32,128]{3,2,1,0:T(8,128)(2,1)} %bitcast.2), custom_call_target="tpu_custom_call" | custom-call | tf_op jit(solution)/shard_map/product/pallas_call | solution.py:197
  23.4 11.9 %all_to_all.11.prod_ref = bf16[32,16,128]{2,1,0:T(8,128)(2,1)} all-to-all(bf16[32,16,128]{2,1,0:T(8,128)(2,1)} %bitcast.3), channel_id=1, replica_groups=mesh['rows'=16,'chan'=2] {'rows','chan'}, dimensions={0} | all-to-all | bytes 262144 | tf_op jit(solution)/shard_map/all_to_all | solution.py:204
  35.3 2.3 %finish.1 = bf16[8,64,128]{2,1,0:T(8,128)(2,1)} custom-call(bf16[32,16,128]{2,1,0:T(8,128)(2,1)} %all_to_all.11.prod_ref, f32[512,128]{1,0:T(8,128)} %get-tuple-element.8.gate_ref, bf16[128,128]{1,0:T(8,128)(2,1)} %w_ref.3), custom_call_target="tpu_custom_call" | custom-call | tf_op jit(solution)/shard_map/finish/pallas_call | solution.py:207

commit v2 on v1

--- a/solution.py
+++ b/solution.py
@@ -10,6 +10,7 @@
 SUBLANES = 8
 EPS = 1e-05
 AXES = ("rows", "chan")
+GRANT = pltpu.CompilerParams(vmem_limit_bytes=4 * 1024 * 1024)
 
 
 def layer_norm(values):
@@ -79,42 +80,44 @@
     return pltpu.roll(values, LANES // 2, values.ndim - 1)
 
 
-def project_kernel(mask_ref, pair_ref, w_ref, out_ref, gate_ref, parts):
+def project_kernel(mask_ref, pair_hbm, w_hbm, out_ref, gate_ref, pair_ref, w_ref, parts, sems):
+    copies = [
+        pltpu.make_async_copy(src, dst, sems.at[at])
+        for at, (src, dst) in enumerate(((pair_hbm, pair_ref), (w_hbm, w_ref)))
+    ]
+    for copy in copies:
+        copy.start()
     rows_dev, cols_dev, width = pair_ref.shape
     tokens, half = rows_dev * cols_dev, width // 2
     row_block = lax.axis_index("rows") * rows_dev // BLOCK
     col_block = lax.axis_index("chan") * cols_dev // BLOCK
+
+    across = (width, width)
+    diagonal = lax.broadcasted_iota(jnp.int32, across, 0) == lax.broadcasted_iota(jnp.int32, across, 1)
+    less_mean = jnp.where(diagonal, 1.0 - 1.0 / width, -1.0 / width).astype(jnp.bfloat16)
+    copies[0].wait()
+    centered = dot_t(less_mean, pair_ref[...].reshape(tokens, width), (1, 1))
+    var = jnp.sum(centered * centered, axis=0, keepdims=True) * (1.0 / width)
+    normed = (centered * lax.rsqrt(var + EPS)).astype(jnp.bfloat16)
+
+    copies[1].wait()
     half_mask = 0.5 * mask_ref[row_block, col_block].astype(jnp.float32)
-
-    pair = pair_ref[...].reshape(tokens, width)
-    ones = jnp.ones((width, width), jnp.bfloat16)
-    mean = jnp.dot(pair, ones, preferred_element_type=jnp.float32) * (1.0 / width)
-    centered = pair.astype(jnp.float32) - mean
-    square = centered * centered
-    high = square.astype(jnp.bfloat16)
-    low = (square - high.astype(jnp.float32)).astype(jnp.bfloat16)
-    total = jnp.dot(high, ones, preferred_element_type=jnp.float32) + jnp.dot(
-        low, ones, preferred_element_type=jnp.float32
-    )
-    normed = (centered * lax.rsqrt(total * (1.0 / width) + EPS)).astype(jnp.bfloat16)
-
     pick = first_half((half, LANES))
+    n_dev, slab = out_ref.shape[0], out_ref.shape[1] // 2
     for side in range(2):
         begin = 2 * side * width
-        gates = dot_t(w_ref[:, begin : begin + width], normed, (0, 1))
-        values = dot_t(w_ref[:, begin + width : begin + 2 * width], normed, (0, 1))
+        gates = dot_t(w_ref[:, begin : begin + width], normed, (0, 0))
+        values = dot_t(w_ref[:, begin + width : begin + 2 * width], normed, (0, 0))
         held = (jnp.tanh(0.5 * gates) * half_mask + half_mask) * values
         for at in range(tokens // LANES):
             low_c = held[:half, at * LANES : (at + 1) * LANES]
             high_c = held[half:, at * LANES : (at + 1) * LANES]
             parts[side, :, 2 * at, :] = jnp.where(pick, low_c, swap(high_c))
             parts[side, :, 2 * at + 1, :] = jnp.where(pick, swap(low_c), high_c)
-    n_dev, slab = out_ref.shape[0], out_ref.shape[1] // 2
-    for side in range(2):
         out_ref[:, side * slab : (side + 1) * slab, :] = (
             parts[side].reshape(n_dev, slab, LANES).astype(jnp.bfloat16)
         )
-    gate = jnp.dot(normed, w_ref[:, 4 * width :], preferred_element_type=jnp.float32)
+    gate = dot_t(w_ref[:, 4 * width :], normed, (0, 0))
     gate_ref[...] = 0.5 * jnp.tanh(0.5 * gate) + 0.5
 
 
@@ -168,9 +171,8 @@
         normed = jnp.concatenate(
             [jnp.where(pick, even, swap(odd)), jnp.where(pick, swap(even), odd)], axis=0
         ).astype(jnp.bfloat16)
-        mixed = dot_t(normed, w, (0, 0))
-        update = gate_ref[at * LANES : (at + 1) * LANES, :] * mixed
-        out_ref[2 * at : 2 * at + 2] = update.astype(jnp.bfloat16).reshape(2, cols_dev, width)
+        update = gate_ref[:, at * LANES : (at + 1) * LANES] * dot_t(w, normed, (0, 0))
+        out_ref[2 * at : 2 * at + 2] = update.astype(jnp.bfloat16).T.reshape(2, cols_dev, width)
 
 
 def vmem():
@@ -186,19 +188,26 @@
         project_kernel,
         out_shape=(
             jax.ShapeDtypeStruct((n_dev, 2 * slab, LANES), jnp.bfloat16),
-            jax.ShapeDtypeStruct((rows_dev * cols_dev, width), jnp.float32),
+            jax.ShapeDtypeStruct((width, rows_dev * cols_dev), jnp.float32),
         ),
-        in_specs=[pl.BlockSpec(memory_space=pltpu.SMEM), vmem(), vmem()],
+        in_specs=[pl.BlockSpec(memory_space=pltpu.SMEM)] + [pl.BlockSpec(memory_space=pltpu.HBM)] * 2,
         out_specs=(vmem(), vmem()),
-        scratch_shapes=[pltpu.VMEM((2, width // 2, SUBLANES, LANES), jnp.float32)],
+        scratch_shapes=[
+            pltpu.VMEM(pair.shape, pair.dtype),
+            pltpu.VMEM(w_in.shape, w_in.dtype),
+            pltpu.VMEM((2, width // 2, SUBLANES, LANES), jnp.float32),
+            pltpu.SemaphoreType.DMA((2,)),
+        ],
+        compiler_params=GRANT,
         name="project",
-    )(block_mask, pair, w_in)
+    )(block_mask, *(pltpu.with_memory_space_constraint(v, pltpu.HBM) for v in (pair, w_in)))
     got = lax.all_to_all(sent, AXES, split_axis=0, concat_axis=0, tiled=True)
     prod = pl.pallas_call(
         product_kernel,
         out_shape=jax.ShapeDtypeStruct((n_rows, n_chan, slab, LANES), jnp.bfloat16),
         in_specs=[vmem()],
         out_specs=vmem(),
+        compiler_params=GRANT,
         name="product",
     )(got.reshape(n_rows, n_chan, 2 * slab, LANES))
     back = lax.all_to_all(
@@ -210,6 +219,7 @@
         in_specs=[vmem()] * 3,
         out_specs=vmem(),
         scratch_shapes=[pltpu.VMEM((width // 2, SUBLANES, LANES), jnp.float32)],
+        compiler_params=GRANT,
         name="finish",
     )(back, gate, w_out)
 

time: 37.9 us -> 32.9 us (0.87)
  Pallas kernels: 6.99 us -> 3.5 us
  blocking collectives: 30 us -> 28.5 us
    pallas_call x1, Pallas kernels: 1.91 us -> 0.3 us  [tiled(): pl.pallas_call(product_kernel, out_shape=jax.ShapeDtypeStruct((n_rows, n_...]
    all_to_all x1, blocking collectives: 11.9 us -> 10.7 us  [tiled(): lax.all_to_all(prod.reshape(n_dev, slab, LANES), AXES, split_axis=0, conc...]
    pallas_call x1, Pallas kernels: 2.32 us -> 1.37 us  [tiled(): pl.pallas_call(finish_kernel, out_shape=jax.ShapeDtypeStruct(pair.shape,...]
    pallas_call x1, Pallas kernels: 2.76 us -> 1.83 us  [tiled(): pl.pallas_call(project_kernel, out_shape=(jax.ShapeDtypeStruct((n_dev, 2...]
where the time goes in v2:
time: 32.9 us; the launch traced here: 32.7 us
  blocking collectives  28.5 us (87%)
  Pallas kernels  3.5 us (11%)
  between operations  0.68 us (2%)
    all_to_all x1, blocking collectives, tiled(): got = lax.all_to_all(sent, AXES, split_axis=0, concat_axis=0, tiled=True)  17.8 us
    all_to_all x1, blocking collectives, tiled(): lax.all_to_all(prod.reshape(n_dev, slab, LANES), AXES, split_axis=0, conc...  10.7 us
    pallas_call x1, Pallas kernels, tiled(): pl.pallas_call(project_kernel, out_shape=(jax.ShapeDtypeStruct((n_dev, 2...  1.83 us
    pallas_call x1, Pallas kernels, tiled(): pl.pallas_call(finish_kernel, out_shape=jax.ShapeDtypeStruct(pair.shape,...  1.37 us

profile of v2, /device:TPU:0, one launch (start us, length us, event | category | flops | bytes accessed | tf_op | source)
XLA Modules:
  0.0 32.7 jit_solution(3231917354465193257)
XLA Ops:
  0.7 1.8 %project.1 = (bf16[32,32,128]{2,1,0:T(8,128)(2,1)S(1)}, f32[128,512]{1,0:T(8,128)S(1)}) custom-call(s32[1,1]{1,0:T(1,128)S(6)} %copy.5.mask_ref, bf16[8,64,128]{2,1,0:T(8,128)(2,1)} %pair_hbm.1, bf16[128,640]{1,0:T(8,128)(2,1)} %w_hbm.1), custom_call_target="tpu_custom_call" | custom-call | tf_op jit(solution)/shard_map/project/pallas_call | solution.py:187
  2.5 17.8 %all_to_all.10 = bf16[32,32,128]{2,1,0:T(8,128)(2,1)S(1)} all-to-all(bf16[32,32,128]{2,1,0:T(8,128)(2,1)S(1)} %get-tuple-element.7), channel_id=1, replica_groups=mesh['rows'=16,'chan'=2] {'rows','chan'}, dimensions={0} | all-to-all | bytes 524288 | tf_op jit(solution)/shard_map/all_to_all | solution.py:204
  20.3 0.3 product.1
  20.6 0.0 copy-start
  20.6 10.7 %all_to_all.11.prod_ref = bf16[32,16,128]{2,1,0:T(8,128)(2,1)S(1)} all-to-all(bf16[32,16,128]{2,1,0:T(8,128)(2,1)S(1)} %bitcast.3), channel_id=1, replica_groups=mesh['rows'=16,'chan'=2] {'rows','chan'}, dimensions={0} | all-to-all | bytes 262144 | tf_op jit(solution)/shard_map/all_to_all | solution.py:213
  31.4 0.0 copy-done
  31.4 1.4 %finish.1 = bf16[8,64,128]{2,1,0:T(8,128)(2,1)} custom-call(bf16[32,16,128]{2,1,0:T(8,128)(2,1)S(1)} %all_to_all.11.prod_ref, f32[128,512]{1,0:T(8,128)S(1)} %get-tuple-element.8.gate_ref, bf16[128,128]{1,0:T(8,128)(2,1)S(1)} %copy-done), custom_call_target="tpu_custom_call" | custom-call | tf_op jit(solution)/shard_map/finish/pallas_call | solution.py:216
Async XLA Ops:
  20.6 10.8 %copy-start = (bf16[128,128]{1,0:T(8,128)(2,1)S(1)}, bf16[128,128]{1,0:T(8,128)(2,1)}, u32[]{:S(2)}) copy-start(bf16[128,128]{1,0:T(8,128)(2,1)} %w_ref.1) | copy-start | bytes 98308

commit v3 on v2

--- a/solution.py
+++ b/solution.py
@@ -1,3 +1,5 @@
+import functools
+
 import jax
 import jax.numpy as jnp
 from jax import lax
@@ -121,14 +123,14 @@
     gate_ref[...] = 0.5 * jnp.tanh(0.5 * gate) + 0.5
 
 
-def product_kernel(in_ref, out_ref):
-    n_rows, n_chan, slabs, _ = in_ref.shape
-    slab = slabs // 2
+def product_kernel(n_rows, n_chan, spots, in_ref, out_ref):
+    slab = out_ref.shape[1]
     groups = slab // SUBLANES
     tokens = n_rows * SUBLANES
 
     def side(at):
-        values = in_ref[:, :, at * slab : (at + 1) * slab, :].astype(jnp.float32)
+        values = in_ref[:, at * slab : (at + 1) * slab, :].astype(jnp.float32)
+        values = jnp.stack([values[spot] for spot in spots])
         return values.reshape(n_rows, n_chan, groups, SUBLANES, LANES)
 
     left, right = side(0), side(1)
@@ -151,7 +153,9 @@
     ]
     for x in range(n_chan):
         block = jnp.concatenate([v.reshape(n_rows, SUBLANES, LANES) for v in blocks[x]], axis=1)
-        out_ref[:, x] = block.astype(jnp.bfloat16)
+        block = block.astype(jnp.bfloat16)
+        for row in range(n_rows):
+            out_ref[spots[row * n_chan + x]] = block[row]
 
 
 def finish_kernel(prod_ref, gate_ref, w_ref, out_ref, parts):
@@ -179,11 +183,24 @@
     return pl.BlockSpec(memory_space=pltpu.VMEM)
 
 
+def exchange_order(n_dev):
+    stride = n_dev // 8 * 2 + 1
+    return [place * stride % n_dev for place in range(n_dev)]
+
+
+def exchange(values, order):
+    return lax.all_to_all(
+        values, AXES, split_axis=0, concat_axis=0, axis_index_groups=[order], tiled=True
+    )
+
+
 def tiled(n_rows, n_chan, pair, block_mask, w_in, w_out):
     rows_dev, cols_dev, width = pair.shape
     n_dev = n_rows * n_chan
     groups = width // (2 * n_dev)
     slab = groups * SUBLANES
+    order = exchange_order(n_dev)
+    spots = [order.index(device) for device in range(n_dev)]
     sent, gate = pl.pallas_call(
         project_kernel,
         out_shape=(
@@ -201,18 +218,16 @@
         compiler_params=GRANT,
         name="project",
     )(block_mask, *(pltpu.with_memory_space_constraint(v, pltpu.HBM) for v in (pair, w_in)))
-    got = lax.all_to_all(sent, AXES, split_axis=0, concat_axis=0, tiled=True)
+    got = exchange(sent, order)
     prod = pl.pallas_call(
-        product_kernel,
-        out_shape=jax.ShapeDtypeStruct((n_rows, n_chan, slab, LANES), jnp.bfloat16),
+        functools.partial(product_kernel, n_rows, n_chan, spots),
+        out_shape=jax.ShapeDtypeStruct((n_dev, slab, LANES), jnp.bfloat16),
         in_specs=[vmem()],
         out_specs=vmem(),
         compiler_params=GRANT,
         name="product",
-    )(got.reshape(n_rows, n_chan, 2 * slab, LANES))
-    back = lax.all_to_all(
-        prod.reshape(n_dev, slab, LANES), AXES, split_axis=0, concat_axis=0, tiled=True
-    )
+    )(got)
+    back = exchange(prod, order)
     return pl.pallas_call(
         finish_kernel,
         out_shape=jax.ShapeDtypeStruct(pair.shape, jnp.bfloat16),

time: 32.9 us -> 31.6 us (0.960)
  blocking collectives: 28.5 us -> 27.2 us
    all_to_all x2, blocking collectives: 28.5 us -> 27.2 us  [exchange(): lax.all_to_all(values, AXES, split_axis=0, concat_axis=0, axis_index_grou...]
where the time goes in v3:
time: 31.6 us; the launch traced here: 31.4 us
  blocking collectives  27.2 us (86%)
  Pallas kernels  3.5 us (11%)
  between operations  0.68 us (2%)
    all_to_all x2, blocking collectives, exchange(): lax.all_to_all(values, AXES, split_axis=0, concat_axis=0, axis_index_grou...  27.2 us
    pallas_call x1, Pallas kernels, tiled(): pl.pallas_call(project_kernel, out_shape=(jax.ShapeDtypeStruct((n_dev, 2...  1.83 us
    pallas_call x1, Pallas kernels, tiled(): pl.pallas_call(finish_kernel, out_shape=jax.ShapeDtypeStruct(pair.shape,...  1.37 us

profile of v3, /device:TPU:0, one launch (start us, length us, event | category | flops | bytes accessed | tf_op | source)
XLA Modules:
  0.0 31.4 jit_solution(6133108870997582194)
XLA Ops:
  0.7 1.8 %project.1 = (bf16[32,32,128]{2,1,0:T(8,128)(2,1)S(1)}, f32[128,512]{1,0:T(8,128)S(1)}) custom-call(s32[1,1]{1,0:T(1,128)S(6)} %copy.5.mask_ref, bf16[8,64,128]{2,1,0:T(8,128)(2,1)} %pair_hbm.1, bf16[128,640]{1,0:T(8,128)(2,1)} %w_hbm.1), custom_call_target="tpu_custom_call" | custom-call | tf_op jit(solution)/shard_map/project/pallas_call | solution.py:204
  2.5 16.9 %all_to_all.10.in_ref = bf16[32,32,128]{2,1,0:T(8,128)(2,1)S(1)} all-to-all(bf16[32,32,128]{2,1,0:T(8,128)(2,1)S(1)} %get-tuple-element.7), channel_id=1, replica_groups={{0,9,18,27,4,13,22,31,8,17,26,3,12,21,30,7,16,25,2,11,20,29,6,15,24,1,1..., dimensions={0} | all-to-all | bytes 524288 | tf_op jit(solution)/shard_map/all_to_all | solution.py:192
  19.4 0.3 product.1
  19.7 0.0 copy-start
  19.7 10.3 %all_to_all.11.prod_ref = bf16[32,16,128]{2,1,0:T(8,128)(2,1)S(1)} all-to-all(bf16[32,16,128]{2,1,0:T(8,128)(2,1)S(1)} %product.1), channel_id=1, replica_groups={{0,9,18,27,4,13,22,31,8,17,26,3,12,21,30,7,16,25,2,11,20,29,6,15,24,1,1..., dimensions={0} | all-to-all | bytes 262144 | tf_op jit(solution)/shard_map/all_to_all | solution.py:192
  30.0 0.0 copy-done
  30.0 1.4 %finish.1 = bf16[8,64,128]{2,1,0:T(8,128)(2,1)} custom-call(bf16[32,16,128]{2,1,0:T(8,128)(2,1)S(1)} %all_to_all.11.prod_ref, f32[128,512]{1,0:T(8,128)S(1)} %get-tuple-element.8.gate_ref, bf16[128,128]{1,0:T(8,128)(2,1)S(1)} %copy-done), custom_call_target="tpu_custom_call" | custom-call | tf_op jit(solution)/shard_map/finish/pallas_call | solution.py:231
Async XLA Ops:
  19.7 10.3 %copy-start = (bf16[128,128]{1,0:T(8,128)(2,1)S(1)}, bf16[128,128]{1,0:T(8,128)(2,1)}, u32[]{:S(2)}) copy-start(bf16[128,128]{1,0:T(8,128)(2,1)} %w_ref.1) | copy-start | bytes 98308

commit v4 on v3

--- a/solution.py
+++ b/solution.py
@@ -82,7 +82,7 @@
     return pltpu.roll(values, LANES // 2, values.ndim - 1)
 
 
-def project_kernel(mask_ref, pair_hbm, w_hbm, out_ref, gate_ref, pair_ref, w_ref, parts, sems):
+def project_kernel(owned, mask_ref, pair_hbm, w_hbm, out_ref, gate_ref, pair_ref, w_ref, parts, sems):
     copies = [
         pltpu.make_async_copy(src, dst, sems.at[at])
         for at, (src, dst) in enumerate(((pair_hbm, pair_ref), (w_hbm, w_ref)))
@@ -116,9 +116,9 @@
             high_c = held[half:, at * LANES : (at + 1) * LANES]
             parts[side, :, 2 * at, :] = jnp.where(pick, low_c, swap(high_c))
             parts[side, :, 2 * at + 1, :] = jnp.where(pick, swap(low_c), high_c)
-        out_ref[:, side * slab : (side + 1) * slab, :] = (
-            parts[side].reshape(n_dev, slab, LANES).astype(jnp.bfloat16)
-        )
+        block = parts[side].reshape(n_dev, slab, LANES).astype(jnp.bfloat16)
+        for place, group in enumerate(owned):
+            out_ref[place, side * slab : (side + 1) * slab, :] = block[group]
     gate = dot_t(w_ref[:, 4 * width :], normed, (0, 0))
     gate_ref[...] = 0.5 * jnp.tanh(0.5 * gate) + 0.5
 
@@ -130,7 +130,7 @@
 
     def side(at):
         values = in_ref[:, at * slab : (at + 1) * slab, :].astype(jnp.float32)
-        values = jnp.stack([values[spot] for spot in spots])
+        values = jnp.stack([values[spot] for spot in spots[0]])
         return values.reshape(n_rows, n_chan, groups, SUBLANES, LANES)
 
     left, right = side(0), side(1)
@@ -155,7 +155,7 @@
         block = jnp.concatenate([v.reshape(n_rows, SUBLANES, LANES) for v in blocks[x]], axis=1)
         block = block.astype(jnp.bfloat16)
         for row in range(n_rows):
-            out_ref[spots[row * n_chan + x]] = block[row]
+            out_ref[spots[1][row * n_chan + x]] = block[row]
 
 
 def finish_kernel(prod_ref, gate_ref, w_ref, out_ref, parts):
@@ -183,9 +183,18 @@
     return pl.BlockSpec(memory_space=pltpu.VMEM)
 
 
-def exchange_order(n_dev):
+def orders(n_rows, n_chan):
+    n_dev = n_rows * n_chan
+    quarter = max(n_rows // 4, 1)
+    there = [
+        (row + at) * n_chan + x
+        for x in range(n_chan)
+        for at in range(quarter)
+        for row in range(n_rows - quarter, -1, -quarter)
+    ]
     stride = n_dev // 8 * 2 + 1
-    return [place * stride % n_dev for place in range(n_dev)]
+    back = [place * stride % n_dev for place in range(n_dev)]
+    return there, back
 
 
 def exchange(values, order):
@@ -199,10 +208,11 @@
     n_dev = n_rows * n_chan
     groups = width // (2 * n_dev)
     slab = groups * SUBLANES
-    order = exchange_order(n_dev)
-    spots = [order.index(device) for device in range(n_dev)]
+    there, back = orders(n_rows, n_chan)
+    owned = [back.index(device) for device in there]
+    spots = [[order.index(device) for device in range(n_dev)] for order in (there, back)]
     sent, gate = pl.pallas_call(
-        project_kernel,
+        functools.partial(project_kernel, owned),
         out_shape=(
             jax.ShapeDtypeStruct((n_dev, 2 * slab, LANES), jnp.bfloat16),
             jax.ShapeDtypeStruct((width, rows_dev * cols_dev), jnp.float32),
@@ -218,7 +228,7 @@
         compiler_params=GRANT,
         name="project",
     )(block_mask, *(pltpu.with_memory_space_constraint(v, pltpu.HBM) for v in (pair, w_in)))
-    got = exchange(sent, order)
+    got = exchange(sent, there)
     prod = pl.pallas_call(
         functools.partial(product_kernel, n_rows, n_chan, spots),
         out_shape=jax.ShapeDtypeStruct((n_dev, slab, LANES), jnp.bfloat16),
@@ -227,7 +237,7 @@
         compiler_params=GRANT,
         name="product",
     )(got)
-    back = exchange(prod, order)
+    returned = exchange(prod, back)
     return pl.pallas_call(
         finish_kernel,
         out_shape=jax.ShapeDtypeStruct(pair.shape, jnp.bfloat16),
@@ -236,7 +246,7 @@
         scratch_shapes=[pltpu.VMEM((width // 2, SUBLANES, LANES), jnp.float32)],
         compiler_params=GRANT,
         name="finish",
-    )(back, gate, w_out)
+    )(returned, gate, w_out)
 
 
 def solution(mesh):

time: 31.6 us -> 31.2 us (0.987)
  blocking collectives: 27.2 us -> 26.8 us
    all_to_all x2, blocking collectives: 27.2 us -> 26.8 us  [exchange(): lax.all_to_all(values, AXES, split_axis=0, concat_axis=0, axis_index_grou...]
where the time goes in v4:
time: 31.2 us; the launch traced here: 31 us
  blocking collectives  26.8 us (86%)
  Pallas kernels  3.5 us (11%)
  between operations  0.68 us (2%)
    all_to_all x2, blocking collectives, exchange(): lax.all_to_all(values, AXES, split_axis=0, concat_axis=0, axis_index_grou...  26.8 us
    pallas_call x1, Pallas kernels, tiled(): pl.pallas_call(functools.partial(project_kernel, owned), out_shape=(jax.S...  1.83 us
    pallas_call x1, Pallas kernels, tiled(): pl.pallas_call(finish_kernel, out_shape=jax.ShapeDtypeStruct(pair.shape,...  1.37 us

profile of v4, /device:TPU:0, one launch (start us, length us, event | category | flops | bytes accessed | tf_op | source)
XLA Modules:
  0.0 31.0 jit_solution(13639268445303082253)
XLA Ops:
  0.7 1.8 %project.1 = (bf16[32,32,128]{2,1,0:T(8,128)(2,1)S(1)}, f32[128,512]{1,0:T(8,128)S(1)}) custom-call(s32[1,1]{1,0:T(1,128)S(6)} %copy.5.mask_ref, bf16[8,64,128]{2,1,0:T(8,128)(2,1)} %pair_hbm.1, bf16[128,640]{1,0:T(8,128)(2,1)} %w_hbm.1), custom_call_target="tpu_custom_call" | custom-call | tf_op jit(solution)/shard_map/project/pallas_call | solution.py:214
  2.5 17.8 %all_to_all.10.in_ref = bf16[32,32,128]{2,1,0:T(8,128)(2,1)S(1)} all-to-all(bf16[32,32,128]{2,1,0:T(8,128)(2,1)S(1)} %get-tuple-element.7), channel_id=1, replica_groups={{24,16,8,0,26,18,10,2,28,20,12,4,30,22,14,6,25,17,9,1,27,19,11,3,29,21,..., dimensions={0} | all-to-all | bytes 524288 | tf_op jit(solution)/shard_map/all_to_all | solution.py:201
  20.3 0.3 product.1
  20.6 0.0 copy-start
  20.6 9.0 %all_to_all.11.prod_ref = bf16[32,16,128]{2,1,0:T(8,128)(2,1)S(1)} all-to-all(bf16[32,16,128]{2,1,0:T(8,128)(2,1)S(1)} %product.1), channel_id=1, replica_groups={{0,9,18,27,4,13,22,31,8,17,26,3,12,21,30,7,16,25,2,11,20,29,6,15,24,1,1..., dimensions={0} | all-to-all | bytes 262144 | tf_op jit(solution)/shard_map/all_to_all | solution.py:201
  29.6 0.0 copy-done
  29.6 1.4 %finish.1 = bf16[8,64,128]{2,1,0:T(8,128)(2,1)} custom-call(bf16[32,16,128]{2,1,0:T(8,128)(2,1)S(1)} %all_to_all.11.prod_ref, f32[128,512]{1,0:T(8,128)S(1)} %get-tuple-element.8.gate_ref, bf16[128,128]{1,0:T(8,128)(2,1)S(1)} %copy-done), custom_call_target="tpu_custom_call" | custom-call | tf_op jit(solution)/shard_map/finish/pallas_call | solution.py:241
Async XLA Ops:
  20.6 9.0 %copy-start = (bf16[128,128]{1,0:T(8,128)(2,1)S(1)}, bf16[128,128]{1,0:T(8,128)(2,1)}, u32[]{:S(2)}) copy-start(bf16[128,128]{1,0:T(8,128)(2,1)} %w_ref.1) | copy-start | bytes 98308

commit v5 on v4

--- a/solution.py
+++ b/solution.py
@@ -162,20 +162,27 @@
     n_dev, slab, _ = prod_ref.shape
     rows_dev, cols_dev, width = out_ref.shape
     prod = prod_ref[...].astype(jnp.float32).reshape(n_dev * slab // SUBLANES, SUBLANES, LANES)
+    parts[...] = prod
+    w = w_ref[...]
+    sums = dot_t(w, jnp.ones((width, LANES), jnp.bfloat16), (0, 0))
     total = jnp.sum(prod, axis=0)
     mean = (total + swap(total)) * (1.0 / width)
     centered = prod - mean
     total = jnp.sum(centered * centered, axis=0)
-    var = (total + swap(total)) * (1.0 / width)
-    parts[...] = centered * lax.rsqrt(var + EPS)
+    scale = lax.rsqrt((total + swap(total)) * (1.0 / width) + EPS)
+
     pick = first_half((width // 2, LANES))
-    w = w_ref[...]
+    pick_row = first_half((1, LANES))
     for at in range(rows_dev // 2):
         even, odd = parts[:, 2 * at, :], parts[:, 2 * at + 1, :]
-        normed = jnp.concatenate(
+        held = jnp.concatenate(
             [jnp.where(pick, even, swap(odd)), jnp.where(pick, swap(even), odd)], axis=0
         ).astype(jnp.bfloat16)
-        update = gate_ref[:, at * LANES : (at + 1) * LANES] * dot_t(w, normed, (0, 0))
+        row_mean, row_scale = (
+            jnp.where(pick_row, v[2 * at : 2 * at + 1], v[2 * at + 1 : 2 * at + 2]) for v in (mean, scale)
+        )
+        mixed = (dot_t(w, held, (0, 0)) - sums * row_mean) * row_scale
+        update = gate_ref[:, at * LANES : (at + 1) * LANES] * mixed
         out_ref[2 * at : 2 * at + 2] = update.astype(jnp.bfloat16).T.reshape(2, cols_dev, width)
 
 

time: 31.2 us -> 31 us (level)
  no operation moved by 1% of the time
where the time goes in v5:
time: 31 us; the launch traced here: 30.8 us
  blocking collectives  26.8 us (86%)
  Pallas kernels  3.3 us (11%)
  between operations  0.68 us (2%)
    all_to_all x2, blocking collectives, exchange(): lax.all_to_all(values, AXES, split_axis=0, concat_axis=0, axis_index_grou...  26.8 us
    pallas_call x1, Pallas kernels, tiled(): pl.pallas_call(functools.partial(project_kernel, owned), out_shape=(jax.S...  1.83 us
    pallas_call x1, Pallas kernels, tiled(): pl.pallas_call(finish_kernel, out_shape=jax.ShapeDtypeStruct(pair.shape,...  1.16 us

profile of v5, /device:TPU:0, one launch (start us, length us, event | category | flops | bytes accessed | tf_op | source)
XLA Modules:
  0.0 30.8 jit_solution(2162819385529784166)
XLA Ops:
  0.7 1.8 %project.1 = (bf16[32,32,128]{2,1,0:T(8,128)(2,1)S(1)}, f32[128,512]{1,0:T(8,128)S(1)}) custom-call(s32[1,1]{1,0:T(1,128)S(6)} %copy.5.mask_ref, bf16[8,64,128]{2,1,0:T(8,128)(2,1)} %pair_hbm.1, bf16[128,640]{1,0:T(8,128)(2,1)} %w_hbm.1), custom_call_target="tpu_custom_call" | custom-call | tf_op jit(solution)/shard_map/project/pallas_call | solution.py:221
  2.5 17.8 %all_to_all.10.in_ref = bf16[32,32,128]{2,1,0:T(8,128)(2,1)S(1)} all-to-all(bf16[32,32,128]{2,1,0:T(8,128)(2,1)S(1)} %get-tuple-element.7), channel_id=1, replica_groups={{24,16,8,0,26,18,10,2,28,20,12,4,30,22,14,6,25,17,9,1,27,19,11,3,29,21,..., dimensions={0} | all-to-all | bytes 524288 | tf_op jit(solution)/shard_map/all_to_all | solution.py:208
  20.3 0.3 product.1
  20.6 0.0 copy-start
  20.6 9.0 %all_to_all.11.prod_ref = bf16[32,16,128]{2,1,0:T(8,128)(2,1)S(1)} all-to-all(bf16[32,16,128]{2,1,0:T(8,128)(2,1)S(1)} %product.1), channel_id=1, replica_groups={{0,9,18,27,4,13,22,31,8,17,26,3,12,21,30,7,16,25,2,11,20,29,6,15,24,1,1..., dimensions={0} | all-to-all | bytes 262144 | tf_op jit(solution)/shard_map/all_to_all | solution.py:208
  29.6 0.0 copy-done
  29.6 1.2 %finish.1 = bf16[8,64,128]{2,1,0:T(8,128)(2,1)} custom-call(bf16[32,16,128]{2,1,0:T(8,128)(2,1)S(1)} %all_to_all.11.prod_ref, f32[128,512]{1,0:T(8,128)S(1)} %get-tuple-element.8.gate_ref, bf16[128,128]{1,0:T(8,128)(2,1)S(1)} %copy-done), custom_call_target="tpu_custom_call" | custom-call | tf_op jit(solution)/shard_map/finish/pallas_call | solution.py:248
Async XLA Ops:
  20.6 9.0 %copy-start = (bf16[128,128]{1,0:T(8,128)(2,1)S(1)}, bf16[128,128]{1,0:T(8,128)(2,1)}, u32[]{:S(2)}) copy-start(bf16[128,128]{1,0:T(8,128)(2,1)} %w_ref.1) | copy-start | bytes 98308

commit v6 on v5

--- a/solution.py
+++ b/solution.py
@@ -82,7 +82,7 @@
     return pltpu.roll(values, LANES // 2, values.ndim - 1)
 
 
-def project_kernel(owned, mask_ref, pair_hbm, w_hbm, out_ref, gate_ref, pair_ref, w_ref, parts, sems):
+def project_kernel(owned, mask_ref, pair_hbm, w_hbm, out_ref, gate_ref, pair_ref, w_ref, sems):
     copies = [
         pltpu.make_async_copy(src, dst, sems.at[at])
         for at, (src, dst) in enumerate(((pair_hbm, pair_ref), (w_hbm, w_ref)))
@@ -111,12 +111,14 @@
         gates = dot_t(w_ref[:, begin : begin + width], normed, (0, 0))
         values = dot_t(w_ref[:, begin + width : begin + 2 * width], normed, (0, 0))
         held = (jnp.tanh(0.5 * gates) * half_mask + half_mask) * values
+        by_row = []
         for at in range(tokens // LANES):
             low_c = held[:half, at * LANES : (at + 1) * LANES]
             high_c = held[half:, at * LANES : (at + 1) * LANES]
-            parts[side, :, 2 * at, :] = jnp.where(pick, low_c, swap(high_c))
-            parts[side, :, 2 * at + 1, :] = jnp.where(pick, swap(low_c), high_c)
-        block = parts[side].reshape(n_dev, slab, LANES).astype(jnp.bfloat16)
+            by_row.append(jnp.where(pick, low_c, swap(high_c)))
+            by_row.append(jnp.where(pick, swap(low_c), high_c))
+        block = pltpu.einshape("icl->cil", jnp.stack(by_row))
+        block = block.reshape(n_dev, slab, LANES).astype(jnp.bfloat16)
         for place, group in enumerate(owned):
             out_ref[place, side * slab : (side + 1) * slab, :] = block[group]
     gate = dot_t(w_ref[:, 4 * width :], normed, (0, 0))
@@ -158,11 +160,11 @@
             out_ref[spots[1][row * n_chan + x]] = block[row]
 
 
-def finish_kernel(prod_ref, gate_ref, w_ref, out_ref, parts):
+def finish_kernel(prod_ref, gate_ref, w_ref, out_ref):
     n_dev, slab, _ = prod_ref.shape
     rows_dev, cols_dev, width = out_ref.shape
     prod = prod_ref[...].astype(jnp.float32).reshape(n_dev * slab // SUBLANES, SUBLANES, LANES)
-    parts[...] = prod
+    by_row = pltpu.einshape("cil->icl", prod)
     w = w_ref[...]
     sums = dot_t(w, jnp.ones((width, LANES), jnp.bfloat16), (0, 0))
     total = jnp.sum(prod, axis=0)
@@ -174,7 +176,7 @@
     pick = first_half((width // 2, LANES))
     pick_row = first_half((1, LANES))
     for at in range(rows_dev // 2):
-        even, odd = parts[:, 2 * at, :], parts[:, 2 * at + 1, :]
+        even, odd = by_row[2 * at], by_row[2 * at + 1]
         held = jnp.concatenate(
             [jnp.where(pick, even, swap(odd)), jnp.where(pick, swap(even), odd)], axis=0
         ).astype(jnp.bfloat16)
@@ -229,7 +231,6 @@
         scratch_shapes=[
             pltpu.VMEM(pair.shape, pair.dtype),
             pltpu.VMEM(w_in.shape, w_in.dtype),
-            pltpu.VMEM((2, width // 2, SUBLANES, LANES), jnp.float32),
             pltpu.SemaphoreType.DMA((2,)),
         ],
         compiler_params=GRANT,
@@ -250,7 +251,6 @@
         out_shape=jax.ShapeDtypeStruct(pair.shape, jnp.bfloat16),
         in_specs=[vmem()] * 3,
         out_specs=vmem(),
-        scratch_shapes=[pltpu.VMEM((width // 2, SUBLANES, LANES), jnp.float32)],
         compiler_params=GRANT,
         name="finish",
     )(returned, gate, w_out)

time: 31 us -> 30.7 us (level)
  no operation moved by 1% of the time
where the time goes in v6:
time: 30.7 us; the launch traced here: 30.5 us
  blocking collectives  26.8 us (87%)
  Pallas kernels  2.99 us (10%)
  between operations  0.68 us (2%)
    all_to_all x2, blocking collectives, exchange(): lax.all_to_all(values, AXES, split_axis=0, concat_axis=0, axis_index_grou...  26.8 us
    pallas_call x1, Pallas kernels, tiled(): pl.pallas_call(functools.partial(project_kernel, owned), out_shape=(jax.S...  1.62 us
    pallas_call x1, Pallas kernels, tiled(): pl.pallas_call(finish_kernel, out_shape=jax.ShapeDtypeStruct(pair.shape,...  1.08 us

profile of v6, /device:TPU:0, one launch (start us, length us, event | category | flops | bytes accessed | tf_op | source)
XLA Modules:
  0.0 30.5 jit_solution(5482080041134352702)
XLA Ops:
  0.7 1.6 %project.1 = (bf16[32,32,128]{2,1,0:T(8,128)(2,1)S(1)}, f32[128,512]{1,0:T(8,128)S(1)}) custom-call(s32[1,1]{1,0:T(1,128)S(6)} %copy.5.mask_ref, bf16[8,64,128]{2,1,0:T(8,128)(2,1)} %pair_hbm.1, bf16[128,640]{1,0:T(8,128)(2,1)} %w_hbm.1), custom_call_target="tpu_custom_call" | custom-call | tf_op jit(solution)/shard_map/project/pallas_call | solution.py:223
  2.3 17.8 %all_to_all.10.in_ref = bf16[32,32,128]{2,1,0:T(8,128)(2,1)S(1)} all-to-all(bf16[32,32,128]{2,1,0:T(8,128)(2,1)S(1)} %get-tuple-element.7), channel_id=1, replica_groups={{24,16,8,0,26,18,10,2,28,20,12,4,30,22,14,6,25,17,9,1,27,19,11,3,29,21,..., dimensions={0} | all-to-all | bytes 524288 | tf_op jit(solution)/shard_map/all_to_all | solution.py:210
  20.1 0.3 product.1
  20.4 0.0 copy-start
  20.4 9.0 %all_to_all.11.prod_ref = bf16[32,16,128]{2,1,0:T(8,128)(2,1)S(1)} all-to-all(bf16[32,16,128]{2,1,0:T(8,128)(2,1)S(1)} %product.1), channel_id=1, replica_groups={{0,9,18,27,4,13,22,31,8,17,26,3,12,21,30,7,16,25,2,11,20,29,6,15,24,1,1..., dimensions={0} | all-to-all | bytes 262144 | tf_op jit(solution)/shard_map/all_to_all | solution.py:210
  29.4 0.0 copy-done
  29.4 1.1 %finish.1 = bf16[8,64,128]{2,1,0:T(8,128)(2,1)} custom-call(bf16[32,16,128]{2,1,0:T(8,128)(2,1)S(1)} %all_to_all.11.prod_ref, f32[128,512]{1,0:T(8,128)S(1)} %get-tuple-element.8.gate_ref, bf16[128,128]{1,0:T(8,128)(2,1)S(1)} %copy-done), custom_call_target="tpu_custom_call" | custom-call | tf_op jit(solution)/shard_map/finish/pallas_call | solution.py:249
Async XLA Ops:
  20.4 9.0 %copy-start = (bf16[128,128]{1,0:T(8,128)(2,1)S(1)}, bf16[128,128]{1,0:T(8,128)(2,1)}, u32[]{:S(2)}) copy-start(bf16[128,128]{1,0:T(8,128)(2,1)} %w_ref.1) | copy-start | bytes 98308

commit v7 on v6

--- a/solution.py
+++ b/solution.py
@@ -111,6 +111,7 @@
         gates = dot_t(w_ref[:, begin : begin + width], normed, (0, 0))
         values = dot_t(w_ref[:, begin + width : begin + 2 * width], normed, (0, 0))
         held = (jnp.tanh(0.5 * gates) * half_mask + half_mask) * values
+        held = held.astype(jnp.bfloat16)
         by_row = []
         for at in range(tokens // LANES):
             low_c = held[:half, at * LANES : (at + 1) * LANES]
@@ -118,7 +119,7 @@
             by_row.append(jnp.where(pick, low_c, swap(high_c)))
             by_row.append(jnp.where(pick, swap(low_c), high_c))
         block = pltpu.einshape("icl->cil", jnp.stack(by_row))
-        block = block.reshape(n_dev, slab, LANES).astype(jnp.bfloat16)
+        block = block.reshape(n_dev, slab, LANES)
         for place, group in enumerate(owned):
             out_ref[place, side * slab : (side + 1) * slab, :] = block[group]
     gate = dot_t(w_ref[:, 4 * width :], normed, (0, 0))

time: 30.7 us -> 30.7 us (level)
  no operation moved by 1% of the time
where the time goes in v7:
time: 30.7 us; the launch traced here: 30.4 us
  blocking collectives  26.8 us (87%)
  Pallas kernels  2.95 us (10%)
  between operations  0.68 us (2%)
    all_to_all x2, blocking collectives, exchange(): lax.all_to_all(values, AXES, split_axis=0, concat_axis=0, axis_index_grou...  26.8 us
    pallas_call x1, Pallas kernels, tiled(): pl.pallas_call(functools.partial(project_kernel, owned), out_shape=(jax.S...  1.57 us
    pallas_call x1, Pallas kernels, tiled(): pl.pallas_call(finish_kernel, out_shape=jax.ShapeDtypeStruct(pair.shape,...  1.08 us

profile of v7, /device:TPU:0, one launch (start us, length us, event | category | flops | bytes accessed | tf_op | source)
XLA Modules:
  0.0 30.4 jit_solution(11744858102385837501)
XLA Ops:
  0.7 1.6 %project.1 = (bf16[32,32,128]{2,1,0:T(8,128)(2,1)S(1)}, f32[128,512]{1,0:T(8,128)S(1)}) custom-call(s32[1,1]{1,0:T(1,128)S(6)} %copy.5.mask_ref, bf16[8,64,128]{2,1,0:T(8,128)(2,1)} %pair_hbm.1, bf16[128,640]{1,0:T(8,128)(2,1)} %w_hbm.1), custom_call_target="tpu_custom_call" | custom-call | tf_op jit(solution)/shard_map/project/pallas_call | solution.py:224
  2.2 17.8 %all_to_all.10.in_ref = bf16[32,32,128]{2,1,0:T(8,128)(2,1)S(1)} all-to-all(bf16[32,32,128]{2,1,0:T(8,128)(2,1)S(1)} %get-tuple-element.7), channel_id=1, replica_groups={{24,16,8,0,26,18,10,2,28,20,12,4,30,22,14,6,25,17,9,1,27,19,11,3,29,21,..., dimensions={0} | all-to-all | bytes 524288 | tf_op jit(solution)/shard_map/all_to_all | solution.py:211
  20.0 0.3 product.1
  20.3 0.0 copy-start
  20.3 9.0 %all_to_all.11.prod_ref = bf16[32,16,128]{2,1,0:T(8,128)(2,1)S(1)} all-to-all(bf16[32,16,128]{2,1,0:T(8,128)(2,1)S(1)} %product.1), channel_id=1, replica_groups={{0,9,18,27,4,13,22,31,8,17,26,3,12,21,30,7,16,25,2,11,20,29,6,15,24,1,1..., dimensions={0} | all-to-all | bytes 262144 | tf_op jit(solution)/shard_map/all_to_all | solution.py:211
  29.4 0.0 copy-done
  29.4 1.1 %finish.1 = bf16[8,64,128]{2,1,0:T(8,128)(2,1)} custom-call(bf16[32,16,128]{2,1,0:T(8,128)(2,1)S(1)} %all_to_all.11.prod_ref, f32[128,512]{1,0:T(8,128)S(1)} %get-tuple-element.8.gate_ref, bf16[128,128]{1,0:T(8,128)(2,1)S(1)} %copy-done), custom_call_target="tpu_custom_call" | custom-call | tf_op jit(solution)/shard_map/finish/pallas_call | solution.py:250
Async XLA Ops:
  20.3 9.0 %copy-start = (bf16[128,128]{1,0:T(8,128)(2,1)S(1)}, bf16[128,128]{1,0:T(8,128)(2,1)}, u32[]{:S(2)}) copy-start(bf16[128,128]{1,0:T(8,128)(2,1)} %w_ref.1) | copy-start | bytes 98308
